TPU v7x, 32 devices: a whole 2x2x4 slice. The times are simulated.
32 devices in a mesh: groups: 2 (over y), tensor: 4 (over z), batch: 4 (over x, core).
Axes of the slice: x: 2, y: 2, z: 4, core: 2. Of those that a mesh axis runs over, the one named last changes fastest.
Arguments:
- latent: bfloat16 [8, 64, 5120], P(('groups', 'batch'), None, 'tensor'), parts along dimension 0, may hold values from -6 to 6
- mod_table: bfloat16 [2, 8, 3, 5120], P(None, None, None, 'tensor'), may hold values from -3 to 3
- skip_layer: int32 [8], P(('groups', 'batch')), parts along dimension 0, may hold values from 0 to 1
- step_index: int32 [8], P(('groups', 'batch')), parts along dimension 0, may hold values from 0 to 7
- up_weight: bfloat16 [2, 5120, 7680], P(None, None, 'tensor'), may hold values from -0.078125 to 0.078125
- down_weight: bfloat16 [2, 7680, 5120], P(None, 'tensor'), may hold values from -0.09375 to 0.09375
- up_in: bfloat16 [2, 5120, 64], P(None, ('tensor', 'batch')), may hold values from -0.75 to 0.75
- up_out: bfloat16 [2, 64, 7680], P(None, None, 'tensor'), may hold values from -0.078125 to 0.078125
- down_in: bfloat16 [2, 7680, 64], P(None, 'tensor'), may hold values from -0.75 to 0.75
- down_out: bfloat16 [2, 64, 5120], P(None, None, ('tensor', 'batch')), may hold values from -0.0625 to 0.0625
Outputs:
- guided: bfloat16 [8, 64, 5120], P(('groups', 'batch'), None, 'tensor'), parts along dimension 0
There are 2 independent parts, one for each index of `groups`. A program takes and returns all parts, laid end to end along the dimension named above; an argument that names none is the same for every part. Nothing has to cross between parts.
All inputs are finite; a program needn't handle non-finite values.
Results may differ from a plain program's by a relative error of at most 0.0082.
Values may be sent and summed in bfloat16 or wider, within the bound.
A program may use at most 320 MiB of HBM per device.

v0:
```python
import jax
import jax.numpy as jnp
from jax import lax
from jax.sharding import PartitionSpec as P

guide_weight = 1.0


def modulate(rows, mod):
    values = rows.astype(jnp.float32)
    center = values - jnp.mean(values, axis=-1, keepdims=True)
    spread = jnp.mean(center * center, axis=-1, keepdims=True)
    normed = center * lax.rsqrt(spread + 1e-06)
    return (normed * (1.0 + mod[1]) + mod[0]).astype(jnp.bfloat16)


def dot32(a, b):
    return jnp.dot(a, b, preferred_element_type=jnp.float32)


def own_columns(array, width):
    start = lax.axis_index("tensor") * width
    return lax.dynamic_slice_in_dim(array, start, width, axis=1)


def hidden_of(rows, mod, w_up, a_own, up_out):
    normed = modulate(rows, mod)
    low = lax.psum(dot32(own_columns(normed, a_own.shape[0]), a_own), "tensor")
    return dot32(normed, w_up) + dot32(low.astype(jnp.bfloat16), up_out)


def project_down(active, w_down, down_in, d_own):
    low = lax.psum(dot32(active, down_in), "tensor")
    total = lax.psum_scatter(dot32(active, w_down), "tensor", scatter_dimension=1, tiled=True)
    return total + dot32(low.astype(jnp.bfloat16), d_own)


def gelu(x):
    return jax.nn.gelu(x, approximate=True)


def per_device(
    latent,
    mod_table,
    skip_layer,
    step_index,
    up_weight,
    down_weight,
    up_in,
    up_out,
    down_in,
    down_out,
):
    tokens = latent[0]
    keep = (skip_layer[0] == 0).astype(jnp.float32)
    mods = lax.dynamic_index_in_dim(mod_table, step_index[0], axis=1, keepdims=False)
    mods_local = mods.astype(jnp.float32)
    a_own = lax.all_gather(up_in, "batch", axis=1, tiled=True)
    d_own = lax.all_gather(down_out, "batch", axis=2, tiled=True)
    tokens_full = lax.all_gather(tokens, "tensor", axis=1, tiled=True)
    mods_full = lax.all_gather(mods[:, :2], "tensor", axis=2, tiled=True).astype(jnp.float32)
    hidden = hidden_of(tokens_full, mods_full[0], up_weight[0], a_own[0], up_out[0])
    active = gelu(hidden).astype(jnp.bfloat16)
    first_sum = project_down(active, down_weight[0], down_in[0], d_own[0])
    token_value = tokens.astype(jnp.float32)
    first = (token_value + mods_local[0, 2] * first_sum).astype(jnp.bfloat16)
    first_full = lax.all_gather(first, "tensor", axis=1, tiled=True)
    count = tokens.shape[0]
    stacked = jnp.concatenate([first_full, tokens_full], axis=0)
    hidden = gelu(hidden_of(stacked, mods_full[1], up_weight[1], a_own[1], up_out[1]))
    active = ((1.0 + guide_weight) * hidden[:count] - (guide_weight * keep) * hidden[count:]).astype(jnp.bfloat16)
    summed = project_down(active, down_weight[1], down_in[1], d_own[1])
    first_value = first.astype(jnp.float32)
    start = first_value + guide_weight * keep * (first_value - token_value)
    return (start + mods_local[1, 2] * summed).astype(jnp.bfloat16)[None]


def solution(mesh):
    placed = (
        P(("groups", "batch"), None, "tensor"),
        P(None, None, None, "tensor"),
        P(("groups", "batch")),
        P(("groups", "batch")),
        P(None, None, "tensor"),
        P(None, "tensor", None),
        P(None, ("tensor", "batch"), None),
        P(None, None, "tensor"),
        P(None, "tensor", None),
        P(None, None, ("tensor", "batch")),
    )
    return jax.shard_map(
        per_device,
        mesh=mesh,
        in_specs=placed,
        out_specs=P(("groups", "batch"), None, "tensor"),
        check_vma=False,
    )
```

profile of v0, /device:TPU:0, one launch (start us, length us, event | category | flops | bytes accessed | tf_op | source)
XLA Modules:
  0.0 216.8 jit_solution(3425057779612896796)
XLA Ops:
  6.5 0.0 copy-start
  6.5 0.0 copy-start.5
  6.5 0.0 reduce-scatter.3.cloned.1.call-start
  7.2 0.2 copy-done
  7.5 14.8 %all_gather.16 = bf16[2,2,5120]{2,0,1:T(2,128)(2,1)S(1)} all-gather(bf16[2,2,1280]{2,0,1:T(2,128)(2,1)S(1)} %slice.95), channel_id=1, replica_groups=mesh['groups'=2,'tensor'=4,'batch'=4] {'tensor'}, dimensions={2}, use_global_device_ids=true | all-gather | bytes 51200 | tf_op jit(solution)/shard_map/all_gather | solution.py:61
  22.5 17.0 %all-gather = bf16[1,64,5120]{2,1,0:T(8,128)(2,1)S(1)} all-gather(bf16[1,64,1280]{2,1,0:T(8,128)(2,1)} %param.10), channel_id=2, replica_groups=mesh['groups'=2,'tensor'=4,'batch'=4] {'tensor'}, dimensions={2}, use_global_device_ids=true | all-gather | bytes 819200 | tf_op jit(solution)/shard_map/all_gather | solution.py:60
  39.4 0.2 convert_reduce_fusion.1
  39.7 0.3 fusion.27
  40.0 0.0 copy-done.5
  40.0 0.2 copy.16
  40.2 7.9 %all_gather.17 = bf16[2,1280,64]{2,0,1:T(2,128)(2,1)S(1)} all-gather(bf16[2,320,64]{2,0,1:T(2,128)(2,1)S(1)} %copy.16), channel_id=1, replica_groups=mesh['groups'=2,'tensor'=4,'batch'=4] {'batch'}, dimensions={1}, use_global_device_ids=true | all-gather | bytes 409600 | tf_op jit(solution)/shard_map/all_gather | solution.py:58
  48.1 0.9 fusion.75
  49.0 0.4 copy.22
  49.4 0.3 fusion.30
  49.7 0.2 fusion.64
  49.9 17.9 %psum.28 = bf16[64,64]{1,0:T(8,128)(2,1)S(1)} all-reduce(f32[64,64]{1,0:T(8,128)S(1)} %fusion.64), channel_id=1, replica_groups=mesh['groups'=2,'tensor'=4,'batch'=4] {'tensor'}, use_global_device_ids=true, to_apply=%region_2.3 | all-reduce | flops 4096 | bytes 24576 | tf_op jit(solution)/shard_map/psum | solution.py:28
  67.8 0.0 copy-start.7
  67.9 8.4 %fusion.6 = f32[64,1920]{1,0:T(8,128)S(1)} fusion(bf16[64,5120]{1,0:T(8,128)(2,1)S(1)} %fusion.30, bf16[2,5120,1920]{2,1,0:T(8,128)(2,1)} %param.14), kind=kOutput, calls=%fused_computation.6 | convolution fusion | flops 1258291200 | bytes 20807680 | tf_op jit(solution)/shard_map/dot_general | solution.py:18
  76.3 0.0 copy-done.7
  76.3 0.3 fusion.45
  76.6 0.0 copy-start.4
  76.6 0.0 copy-start.6
  76.6 11.3 %fusion.4 = f32[64,5120]{1,0:T(8,128)} fusion(bf16[64,1920]{1,0:T(8,128)(2,1)S(1)} %fusion.45, bf16[2,1920,5120]{2,1,0:T(8,128)(2,1)} %param.15), kind=kOutput, calls=%fused_computation.4 | convolution fusion | flops 1258291200 | bytes 21217280 | tf_op jit(solution)/shard_map/dot_general | solution.py:18
  87.9 0.0 copy-done.4
  87.9 0.0 reduce-scatter.3.cloned.1.call-update
  88.0 0.0 copy-start.3
  88.0 0.0 reduce-scatter.5.cloned.1.call-start
  88.0 0.0 copy-done.6
  88.0 0.2 copy.18
  88.2 6.9 %all_gather.18 = bf16[2,64,1280]{1,0,2:T(2,128)(2,1)S(1)} all-gather(bf16[2,64,320]{1,0,2:T(2,128)(2,1)S(1)} %copy.18), channel_id=1, replica_groups=mesh['groups'=2,'tensor'=4,'batch'=4] {'batch'}, dimensions={2}, use_global_device_ids=true | all-gather | bytes 409600 | tf_op jit(solution)/shard_map/all_gather | solution.py:59
  95.1 0.0 copy-start.2
  95.2 0.9 fusion.74
  96.1 0.4 copy.23
  96.5 0.4 copy.24
  97.6 0.0 copy-done.3
  97.6 1.2 fusion.54
  98.7 17.4 %psum.29 = bf16[64,64]{1,0:T(8,128)(2,1)S(1)} all-reduce(f32[64,64]{1,0:T(8,128)S(1)} %fusion.54), channel_id=1, replica_groups=mesh['groups'=2,'tensor'=4,'batch'=4] {'tensor'}, use_global_device_ids=true, to_apply=%region_4.5 | all-reduce | flops 4096 | bytes 24576 | tf_op jit(solution)/shard_map/psum | solution.py:33
  116.2 1.5 reduce-scatter.3.cloned.1.call-done
  117.7 0.0 copy-done.2
  117.7 1.2 fusion.22
  118.9 17.0 %all_gather.19 = bf16[64,5120]{1,0:T(8,128)(2,1)S(1)} all-gather(bf16[64,1280]{1,0:T(8,128)(2,1)S(1)} %fusion.22), channel_id=1, replica_groups=mesh['groups'=2,'tensor'=4,'batch'=4] {'tensor'}, dimensions={1}, use_global_device_ids=true | all-gather | bytes 819200 | tf_op jit(solution)/shard_map/all_gather | solution.py:67
  135.9 0.3 convert_reduce_fusion
  136.2 0.5 fusion.14
  136.7 0.6 fusion.17
  137.3 0.0 copy-start.8
  137.3 10.5 %fusion.2 = f32[128,1920]{1,0:T(8,128)} fusion(bf16[128,5120]{1,0:T(8,128)(2,1)S(1)} %fusion.17, bf16[2,5120,1920]{2,1,0:T(8,128)(2,1)} %param.14), kind=kOutput, calls=%fused_computation.2 | convolution fusion | flops 2516582400 | bytes 21954560 | tf_op jit(solution)/shard_map/dot_general | solution.py:18
  147.8 0.2 fusion.49
  148.0 17.0 %psum.30 = bf16[128,64]{0,1:T(8,128)(2,1)S(1)} all-reduce(f32[128,64]{0,1:T(8,128)S(1)} %fusion.49), channel_id=1, replica_groups=mesh['groups'=2,'tensor'=4,'batch'=4] {'tensor'}, use_global_device_ids=true, to_apply=%region_7.8 | all-reduce | flops 8192 | bytes 49152 | tf_op jit(solution)/shard_map/psum | solution.py:28
  165.0 0.0 copy-done.8
  165.0 1.7 fusion.37
  166.7 0.1 fusion.47
  166.8 0.0 copy-start.1
  166.8 11.3 %fusion = f32[64,5120]{1,0:T(8,128)} fusion(bf16[64,1920]{1,0:T(8,128)(2,1)S(1)} %fusion.47, bf16[2,1920,5120]{2,1,0:T(8,128)(2,1)} %param.15), kind=kOutput, calls=%fused_computation | convolution fusion | flops 1258291200 | bytes 21217280 | tf_op jit(solution)/shard_map/dot_general | solution.py:18
  178.1 0.0 reduce-scatter.5.cloned.1.call-update
  178.1 0.4 copy.25
  178.5 0.2 fusion.51
  178.8 17.1 %psum.31 = bf16[64,64]{1,0:T(8,128)(2,1)S(1)} all-reduce(f32[64,64]{1,0:T(8,128)S(1)} %fusion.51), channel_id=1, replica_groups=mesh['groups'=2,'tensor'=4,'batch'=4] {'tensor'}, use_global_device_ids=true, to_apply=%region_9.10 | all-reduce | flops 4096 | bytes 24576 | tf_op jit(solution)/shard_map/psum | solution.py:33
  195.8 12.3 %reduce-scatter.5.cloned.1.call-done = f32[64,1280]{1,0:T(8,128)} async-done(((f32[64,5120]{1,0:T(8,128)}), f32[64,1280]{1,0:T(8,128)}) %reduce-scatter.5.cloned.1.call-update) | async-done | bytes 327696 | tf_op jit(solution)/shard_map/reduce_scatter | solution.py:34
  208.1 1.8 fusion.24
  210.0 0.0 copy-done.1
  (11 shorter events, 0.2 us)
Async XLA Ops:
  6.5 0.9 copy-start
  6.5 33.5 %copy-start.5 = (bf16[2,320,64]{1,2,0:T(8,128)(2,1)S(1)}, bf16[2,320,64]{1,2,0:T(8,128)(2,1)}, u32[]{:S(2)}) copy-start(bf16[2,320,64]{1,2,0:T(8,128)(2,1)} %param.16) | copy-start | bytes 245764
  6.5 111.2 %reduce-scatter.3.cloned.1.call-start = ((), (), s32[]{:S(2)}) async-start(), calls=%async_computation.2 | async-start | bytes 1638400 | tf_op jit(solution)/shard_map/reduce_scatter | solution.py:34
  67.8 8.4 %copy-start.7 = (bf16[2,64,1920]{2,1,0:T(8,128)(2,1)S(1)}, bf16[2,64,1920]{2,1,0:T(8,128)(2,1)}, u32[]{:S(2)}) copy-start(bf16[2,64,1920]{2,1,0:T(8,128)(2,1)} %param.17) | copy-start | bytes 1474564
  76.6 11.3 %copy-start.4 = (bf16[64,1920]{1,0:T(8,128)(2,1)}, bf16[64,1920]{1,0:T(8,128)(2,1)S(1)}, u32[]{:S(2)}) copy-start(bf16[64,1920]{1,0:T(8,128)(2,1)S(1)} %fusion.45) | copy-start | bytes 737284
  76.6 11.4 %copy-start.6 = (bf16[2,64,320]{2,1,0:T(8,128)(2,1)S(1)}, bf16[2,64,320]{2,1,0:T(8,128)(2,1)}, u32[]{:S(2)}) copy-start(bf16[2,64,320]{2,1,0:T(8,128)(2,1)} %param.19) | copy-start | bytes 245764
  88.0 9.6 %copy-start.3 = (bf16[2,1920,64]{1,2,0:T(8,128)(2,1)S(1)}, bf16[2,1920,64]{1,2,0:T(8,128)(2,1)}, u32[]{:S(2)}) copy-start(bf16[2,1920,64]{1,2,0:T(8,128)(2,1)} %param.18) | copy-start | bytes 1474564
  88.0 120.2 %reduce-scatter.5.cloned.1.call-start = ((), (), s32[]{:S(2)}) async-start(), calls=%async_computation.3 | async-start | bytes 1638400 | tf_op jit(solution)/shard_map/reduce_scatter | solution.py:34
  95.1 22.6 %copy-start.2 = (bf16[1,64,1280]{2,1,0:T(8,128)(2,1)S(1)}, bf16[1,64,1280]{2,1,0:T(8,128)(2,1)}, u32[]{:S(2)}) copy-start(bf16[1,64,1280]{2,1,0:T(8,128)(2,1)} %param.10) | copy-start | bytes 491524
  137.3 27.7 %copy-start.8 = (bf16[2,64,1920]{2,1,0:T(8,128)(2,1)S(1)}, bf16[2,64,1920]{2,1,0:T(8,128)(2,1)}, u32[]{:S(2)}) copy-start(bf16[2,64,1920]{2,1,0:T(8,128)(2,1)} %param.17) | copy-start | bytes 1474564
  166.8 43.2 %copy-start.1 = (bf16[2,8,3,1280]{3,1,2,0:T(8,128)(2,1)S(1)}, bf16[2,8,3,1280]{3,1,2,0:T(8,128)(2,1)}, u32[]{:S(2)}) copy-start(bf16[2,8,3,1280]{3,1,2,0:T(8,128)(2,1)} %param.11) | copy-start | bytes 368644
Sparse Core Ops, SparseCore 0:
  88.1 29.5 reduce-scatter.2
  178.3 29.8 reduce-scatter.4
where the time goes:
time: 217 us
  blocking collectives  133 us (61%)
  matrix products  48.3 us (22%)
  between operations  15 us (7%)
  waiting for transfers between devices  13.9 us (6%)
  local copies, waits for them, and re-layouts  4.16 us (2%)
  other arithmetic  2.4 us (1%)
    dot_general x12, matrix products, dot32(): return jnp.dot(a, b, preferred_element_type=jnp.float32)  48.3 us
    psum x2, blocking collectives, hidden_of(): low = lax.psum(dot32(own_columns(normed, a_own.shape[0]), a_own), 'tensor')  34.9 us
    psum x2, blocking collectives, project_down(): low = lax.psum(dot32(active, down_in), 'tensor')  34.5 us
    all_gather x1, blocking collectives, per_device(): first_full = lax.all_gather(first, 'tensor', axis=1, tiled=True)  17 us
    all_gather x1, blocking collectives, per_device(): tokens_full = lax.all_gather(tokens, 'tensor', axis=1, tiled=True)  17 us
    all_gather x1, blocking collectives, per_device(): lax.all_gather(mods[:, :2], 'tensor', axis=2, tiled=True)  14.8 us
    reduce_scatter x2, waiting for transfers between devices, project_down(): lax.psum_scatter(dot32(active, w_down), 'tensor', scatter_dimension=1, ti...  13.8 us
    all_gather x1, blocking collectives, per_device(): a_own = lax.all_gather(up_in, 'batch', axis=1, tiled=True)  7.89 us
  transfers between devices with their start and end apart: 2, of which 2 were waited for; matrix products, arithmetic and copies ran while one was open for 2% of the time, Pallas kernels for 0%

commit v1 on v0

--- a/solution.py
+++ b/solution.py
@@ -1,6 +1,10 @@
+import functools
+
 import jax
 import jax.numpy as jnp
 from jax import lax
+from jax.experimental import pallas as pl
+from jax.experimental.pallas import tpu as pltpu
 from jax.sharding import PartitionSpec as P
 
 guide_weight = 1.0
@@ -75,6 +79,320 @@
     return (start + mods_local[1, 2] * summed).astype(jnp.bfloat16)[None]
 
 
+T_NAME = "tensor"
+B_NAME = "batch"
+LANES = 128
+
+
+def matmul_tiles(width, tile, body):
+    whole = width // tile
+
+    @pl.loop(0, whole)
+    def _(i):
+        body(pl.multiple_of(i * tile, tile), tile)
+
+    if width % tile:
+        body(whole * tile, width % tile)
+
+
+def moments(values):
+    mean = jnp.mean(values, axis=-1, keepdims=True)
+    center = values - mean
+    return mean, jnp.sum(center * center, axis=-1, keepdims=True)
+
+
+def pack_moments(values):
+    mean, square = moments(values)
+    count = values.shape[0]
+    lane = lax.broadcasted_iota(jnp.int32, (count, LANES), 1)
+    both = jnp.where(lane == 0, mean, jnp.where(lane == 1, square, 0.0))
+    if count < LANES:
+        both = jnp.concatenate([both, jnp.zeros((LANES - count, LANES), jnp.float32)], axis=0)
+    return both.T[:8]
+
+
+def unpack_moments(packed, count):
+    whole = jnp.concatenate([packed, jnp.zeros((LANES - 8, LANES), jnp.float32)], axis=0).T
+    return whole[:count, 0:1], whole[:count, 1:2]
+
+
+def window_kernel(
+    n, nb,
+    keep_ref, lat_ref, mod_ref, gate_ref, ad_ref, uo_ref, di_ref, uw, dw,
+    out_ref,
+    rows_all, mod_all, stat_all, low_all, back_all, ad_all, sums_in, sums_out,
+    normed, act, hid, own, stat_mine, low_mine, back_mine,
+    up_buf, down_buf,
+    up_sem, down_sem,
+    rows_s, rows_r, mod_s, mod_r, stat_s, stat_r, low_s, low_r, back_s, back_r, ad_s, ad_r, sum_s, sum_r,
+):
+    me = lax.axis_index(T_NAME)
+    mb = lax.axis_index(B_NAME)
+    count, width = lat_ref.shape
+    units = uo_ref.shape[1]
+    part = ad_ref.shape[1]
+    up_slots = up_buf.shape[0]
+    lane_rows = width // LANES
+    keep = keep_ref[0]
+    f32, bf16 = jnp.float32, jnp.bfloat16
+
+    def up_copy(level, step):
+        chunk = level * n + step
+        block = lax.rem(me + n - step, n)
+        rows = pl.ds(pl.multiple_of(block * width, LANES), width)
+        return pltpu.make_async_copy(uw.at[level, rows, :], up_buf.at[chunk % up_slots], up_sem.at[chunk])
+
+    def down_copy(level, step):
+        block = lax.rem(me + 1 + step, n)
+        columns = pl.ds(pl.multiple_of(block * width, LANES), width)
+        return pltpu.make_async_copy(dw.at[level, :, columns], down_buf.at[step], down_sem.at[level * n + step])
+
+    for step in range(n):
+        up_copy(0, step).start()
+    for step in range(n):
+        down_copy(0, step).start()
+    for step in range(up_slots - n):
+        up_copy(1, step).start()
+
+    sent = []
+
+    def send(src, dst, s, r, where):
+        copy = pltpu.make_async_remote_copy(
+            src_ref=src, dst_ref=dst, send_sem=s, recv_sem=r,
+            device_id=where, device_id_type=pl.DeviceIdType.MESH)
+        copy.start()
+        sent.append(copy)
+
+    def arrive(buf, r):
+        pltpu.make_async_remote_copy(
+            src_ref=buf, dst_ref=buf, send_sem=r, recv_sem=r,
+            device_id={T_NAME: lax.rem(me + 1, n)}, device_id_type=pl.DeviceIdType.MESH).wait_recv()
+
+    def to_peers(src, dst, s, r):
+        for step in range(1, n):
+            send(src, dst, s.at[step], r.at[me], {T_NAME: lax.rem(me + step, n)})
+
+    def from_peers(buf, r):
+        for step in range(1, n):
+            block = lax.rem(me + n - step, n)
+            arrive(buf.at[block], r.at[block])
+
+    stat_mine[0] = pack_moments(lat_ref[...].astype(f32))
+    barrier = pltpu.get_barrier_semaphore()
+    for step in range(1, n):
+        pl.semaphore_signal(barrier, inc=1, device_id={T_NAME: lax.rem(me + step, n)}, device_id_type=pl.DeviceIdType.MESH)
+    for step in range(1, nb):
+        pl.semaphore_signal(barrier, inc=1, device_id={B_NAME: lax.rem(mb + step, nb)}, device_id_type=pl.DeviceIdType.MESH)
+    pl.semaphore_wait(barrier, n - 1 + nb - 1)
+
+    to_peers(stat_mine.at[0], stat_all.at[0, me], stat_s.at[0], stat_r.at[0])
+    to_peers(mod_ref, mod_all.at[me], mod_s, mod_r)
+    to_peers(lat_ref, rows_all.at[0, me], rows_s.at[0], rows_r.at[0])
+    spot = pl.ds(pl.multiple_of(mb * part, 16), part)
+    for level in range(2):
+        for step in range(1, nb):
+            send(ad_ref.at[level], ad_all.at[level, spot, :], ad_s.at[level, step], ad_r.at[level, mb], {B_NAME: lax.rem(mb + step, nb)})
+    mod_all[me] = mod_ref[...]
+    ad_all[:, spot, :] = ad_ref[...]
+    stat_all[0, me] = stat_mine[0]
+    rows_all[0, me] = lat_ref[...]
+
+    def wait_ad(level):
+        for step in range(1, nb):
+            other = lax.rem(mb + step, nb)
+            there = pl.ds(pl.multiple_of(other * part, 16), part)
+            arrive(ad_all.at[level, there, :], ad_r.at[level, other])
+
+    def statistics(kind):
+        parts = [unpack_moments(stat_all[kind, b], count) for b in range(n)]
+        mean = sum(p[0] for p in parts) * (1.0 / n)
+        square = sum(p[1] + width * (p[0] - mean) * (p[0] - mean) for p in parts)
+        return mean, lax.rsqrt(square * (1.0 / (n * width)) + 1e-06)
+
+    def mod_row(block, row):
+        return jnp.concatenate([mod_all[block, row * lane_rows + j : row * lane_rows + j + 1, :] for j in range(lane_rows)], axis=1)
+
+    def apply(kind, level, block, stats):
+        values = rows_all[kind, block].astype(f32)
+        return ((values - stats[0]) * stats[1] * (1.0 + mod_row(block, 2 * level + 1)) + mod_row(block, 2 * level)).astype(bf16)
+
+    def up_step(slot, target, init):
+        def body(start, size):
+            columns = pl.ds(start, size)
+            value = jnp.dot(normed[...], up_buf[slot, :, columns], preferred_element_type=f32)
+            if init:
+                hid[target, :, columns] = value
+            else:
+                hid[target, :, columns] += value
+
+        matmul_tiles(units, 512, body)
+
+    def add_low(target, low):
+        def body(start, size):
+            columns = pl.ds(start, size)
+            hid[target, :, columns] += jnp.dot(low, uo_ref[:, columns], preferred_element_type=f32)
+
+        matmul_tiles(units, 512, body)
+
+    half = lax.broadcasted_iota(jnp.int32, (count, LANES), 1) < LANES // 2
+
+    def low_sum(kind):
+        return sum(low_all[kind, b] for b in range(n))
+
+    def back_projection(level):
+        value = jnp.dot(act[...], di_ref[...], preferred_element_type=f32)
+        mine = half if level == 1 else jnp.logical_not(half)
+        back_mine[level] = jnp.where(mine, value, 0.0)
+        back_all[level, me] = back_mine[level]
+        to_peers(back_mine.at[level], back_all.at[level, me], back_s.at[level], back_r.at[level])
+
+    def down_steps(level):
+        for step in range(n):
+            down_copy(level, step).wait()
+
+            def body(start, size):
+                columns = pl.ds(start, size)
+                value = jnp.dot(act[...], down_buf[step, :, columns], preferred_element_type=f32)
+                if step < n - 1:
+                    sums_out[level, step, :, columns] = value.astype(bf16)
+                else:
+                    own[:, columns] = value
+
+            matmul_tiles(width, 256, body)
+            if step < n - 1:
+                send(sums_out.at[level, step], sums_in.at[level, me], sum_s.at[level, step], sum_r.at[level, me], {T_NAME: lax.rem(me + 1 + step, n)})
+            if level == 0:
+                down_copy(1, step).start()
+
+    def settle(level):
+        from_peers(back_all.at[level], back_r.at[level])
+        low = sum(back_all[level, b] for b in range(n)).astype(bf16)
+        total = own[...] + lax.dot_general(low, ad_all[level], (((1,), (1,)), ((), ())), preferred_element_type=f32)
+        from_peers(sums_in.at[level], sum_r.at[level])
+        for step in range(1, n):
+            total = total + sums_in[level, lax.rem(me + step, n)].astype(f32)
+        return total
+
+    from_peers(stat_all.at[0], stat_r.at[0])
+    from_peers(mod_all, mod_r)
+    lat_stats = statistics(0)
+    wait_ad(0)
+    low0 = jnp.dot(apply(0, 0, me, lat_stats), ad_all[0], preferred_element_type=f32)
+    wait_ad(1)
+    low1 = jnp.dot(apply(0, 1, me, lat_stats), ad_all[1], preferred_element_type=f32)
+    low_mine[0] = jnp.where(half, low0, low1)
+    low_all[0, me] = low_mine[0]
+    to_peers(low_mine.at[0], low_all.at[0, me], low_s.at[0], low_r.at[0])
+    for step in range(n):
+        block = lax.rem(me + n - step, n)
+        if step:
+            arrive(rows_all.at[0, block], rows_r.at[0, block])
+        normed[...] = apply(0, 0, block, lat_stats)
+        up_copy(0, step).wait()
+        up_step(step, 0, step == 0)
+        later = up_slots - n + step
+        if later < n:
+            up_copy(1, later).start()
+    from_peers(low_all.at[0], low_r.at[0])
+    add_low(0, jnp.where(half, low_sum(0), 0.0).astype(bf16))
+    act[...] = jax.nn.gelu(hid[0], approximate=True).astype(bf16)
+    back_projection(0)
+    down_steps(0)
+    for step in range(n):
+        block = lax.rem(me + n - step, n)
+        normed[...] = apply(0, 1, block, lat_stats)
+        up_copy(1, step).wait()
+        up_step((n + step) % up_slots, 1, step == 0)
+    add_low(1, jnp.where(half, 0.0, low_sum(0)).astype(bf16))
+    hid[1] = jax.nn.gelu(hid[1], approximate=True)
+    first = (lat_ref[...].astype(f32) + gate_ref[0:1, :] * settle(0)).astype(bf16)
+    rows_all[1, me] = first
+    stat_mine[1] = pack_moments(first.astype(f32))
+    to_peers(stat_mine.at[1], stat_all.at[1, me], stat_s.at[1], stat_r.at[1])
+    to_peers(rows_all.at[1, me], rows_all.at[1, me], rows_s.at[1], rows_r.at[1])
+    stat_all[1, me] = stat_mine[1]
+    from_peers(stat_all.at[1], stat_r.at[1])
+    stats = statistics(1)
+    low = jnp.dot(apply(1, 1, me, stats), ad_all[1], preferred_element_type=f32)
+    low_mine[1] = jnp.where(half, 0.0, low)
+    low_all[1, me] = low_mine[1]
+    to_peers(low_mine.at[1], low_all.at[1, me], low_s.at[1], low_r.at[1])
+    for step in range(n):
+        block = lax.rem(me + n - step, n)
+        if step:
+            arrive(rows_all.at[1, block], rows_r.at[1, block])
+        normed[...] = apply(1, 1, block, stats)
+        up_step((n + step) % up_slots, 0, step == 0)
+    from_peers(low_all.at[1], low_r.at[1])
+    add_low(0, low_sum(1).astype(bf16))
+    active = jax.nn.gelu(hid[0], approximate=True)
+    act[...] = ((1.0 + guide_weight) * active - (guide_weight * keep) * hid[1]).astype(bf16)
+    back_projection(1)
+    down_steps(1)
+    total = settle(1)
+    first_value = rows_all[1, me].astype(f32)
+    start = first_value + guide_weight * keep * (first_value - lat_ref[...].astype(f32))
+    out_ref[...] = (start + gate_ref[1:2, :] * total).astype(out_ref.dtype)
+    for copy in sent:
+        copy.wait_send()
+
+
+def per_device_fused(n, nb, latent, mod_table, skip_layer, step_index, up_weight, down_weight, up_in, up_out, down_in, down_out):
+    f32, bf16 = jnp.float32, jnp.bfloat16
+    tokens = latent[0]
+    count, width = tokens.shape
+    units = up_weight.shape[2]
+    keep = (skip_layer == 0).astype(f32)
+    mods = lax.dynamic_index_in_dim(mod_table, step_index[0], axis=1, keepdims=False).astype(f32)
+    lane_rows = 4 * width // LANES
+    mod_packed = mods[:, :2].reshape(lane_rows, LANES)
+    gates = mods[:, 2]
+    turned = jnp.swapaxes(down_out, 1, 2)
+    ad = jnp.stack([jnp.concatenate([up_in[0], turned[0]], axis=1), jnp.concatenate([turned[1], up_in[1]], axis=1)])
+    di = jnp.concatenate([down_in[1], down_in[0]], axis=1)
+    uo = up_out.reshape(LANES, units)
+    up_slots = n + 2
+    vmem = pl.BlockSpec(memory_space=pltpu.VMEM)
+    hbm = pl.BlockSpec(memory_space=pl.ANY)
+    dma = pltpu.SemaphoreType.DMA
+    part = ad.shape[1]
+    return pl.pallas_call(
+        functools.partial(window_kernel, n, nb),
+        out_shape=jax.ShapeDtypeStruct((count, width), bf16),
+        in_specs=[pl.BlockSpec(memory_space=pltpu.SMEM)] + [vmem] * 6 + [hbm] * 2,
+        out_specs=vmem,
+        scratch_shapes=[
+            pltpu.VMEM((2, n, count, width), bf16),
+            pltpu.VMEM((n, lane_rows, LANES), f32),
+            pltpu.VMEM((2, n, 8, LANES), f32),
+            pltpu.VMEM((2, n, count, LANES), f32),
+            pltpu.VMEM((2, n, count, LANES), f32),
+            pltpu.VMEM((2, part * nb, LANES), bf16),
+            pltpu.VMEM((2, n, count, width), bf16),
+            pltpu.VMEM((2, n - 1, count, width), bf16),
+            pltpu.VMEM((count, width), bf16),
+            pltpu.VMEM((count, units), bf16),
+            pltpu.VMEM((2, count, units), f32),
+            pltpu.VMEM((count, width), f32),
+            pltpu.VMEM((2, 8, LANES), f32),
+            pltpu.VMEM((2, count, LANES), f32),
+            pltpu.VMEM((2, count, LANES), f32),
+            pltpu.VMEM((up_slots, width, units), bf16),
+            pltpu.VMEM((n, units, width), bf16),
+            dma((2 * n,)), dma((2 * n,)),
+            dma((2, n)), dma((2, n)),
+            dma((n,)), dma((n,)),
+            dma((2, n)), dma((2, n)),
+            dma((2, n)), dma((2, n)),
+            dma((2, n)), dma((2, n)),
+            dma((2, nb)), dma((2, nb)),
+            dma((2, n)), dma((2, n)),
+        ],
+        compiler_params=pltpu.CompilerParams(collective_id=0, has_side_effects=True, vmem_limit_bytes=63 * 2**20),
+        cost_estimate=pl.CostEstimate(flops=8 * 10**9, bytes_accessed=80 * 10**6, transcendentals=400000),
+    )(keep, tokens, mod_packed, gates, ad, uo, di, up_weight, down_weight)[None]
+
+
 def solution(mesh):
     placed = (
         P(("groups", "batch"), None, "tensor"),
@@ -88,8 +406,20 @@
         P(None, "tensor", None),
         P(None, None, ("tensor", "batch")),
     )
+    n, nb = mesh.shape["tensor"], mesh.shape["batch"]
+
+    def one_device(*arrays):
+        latent, up_weight, up_out = arrays[0], arrays[4], arrays[7]
+        count, width = latent.shape[1:]
+        units, rank = up_weight.shape[2], up_out.shape[1]
+        aligned = width % LANES == 0 and units % LANES == 0 and 2 * rank == LANES
+        small = n * width * units * 2 <= 20 * 2**20 and n > 2 and nb > 1
+        if aligned and small and count % 16 == 0 and count <= LANES:
+            return per_device_fused(n, nb, *arrays)
+        return per_device(*arrays)
+
     return jax.shard_map(
-        per_device,
+        one_device,
         mesh=mesh,
         in_specs=placed,
         out_specs=P(("groups", "batch"), None, "tensor"),

time: 217 us -> 92.9 us (0.43)
  blocking collectives: 133 us -> 0 us
  Pallas kernels: 0 us -> 82.6 us
  matrix products: 48.3 us -> 0 us
  waiting for transfers between devices: 13.9 us -> 0 us
  between operations: 15 us -> 1.4 us
  local copies, waits for them, and re-layouts: 4.16 us -> 6.7 us
    pallas_call x0 -> x1, Pallas kernels: none -> 82.6 us  [per_device_fused(): pl.pallas_call(functools.partial(window_kernel, n, nb), out_shape=jax.Sha...]
    psum x4 -> x0, blocking collectives: 69.4 us -> none  [the longest x2 34.9 us: hidden_of(): low = lax.psum(dot32(own_columns(normed, a_own.shape[0]), a_own), 'tensor')]
    all_gather x5 -> x0, blocking collectives: 63.6 us -> none  [the longest x1 17 us: per_device(): first_full = lax.all_gather(first, 'tensor', axis=1, tiled=True)]
    dot_general x12 -> x0, matrix products: 48.3 us -> none  [dot32(): return jnp.dot(a, b, preferred_element_type=jnp.float32)]
    reduce_scatter x2 -> x0, waiting for transfers between devices: 13.8 us -> none  [project_down(): lax.psum_scatter(dot32(active, w_down), 'tensor', scatter_dimension=1, ti...]
  transfers between devices with their start and end apart: 2 -> 0, of which waited for: 2 -> 0; matrix products, arithmetic and copies ran while one was open for 2% -> 0% of each run, Pallas kernels for 0% -> 0%
where the time goes in v1:
time: 92.9 us; the launch traced here: 92.6 us
  Pallas kernels  82.6 us (89%)
  local copies, waits for them, and re-layouts  6.7 us (7%)
  other arithmetic  1.88 us (2%)
  between operations  1.4 us (2%)
    pallas_call x1, Pallas kernels, per_device_fused(): pl.pallas_call(functools.partial(window_kernel, n, nb), out_shape=jax.Sha...  82.6 us
    unnamed x8, local copies, waits for them, and re-layouts  3.49 us

profile of v1, /device:TPU:0, one launch (start us, length us, event | category | flops | bytes accessed | tf_op | source)
XLA Modules:
  0.0 92.6 jit_solution(11999088547716318598)
XLA Ops:
  0.0 0.0 copy-start
  0.0 1.1 %copy.20 = bf16[2,64,320]{1,2,0:T(8,128)(2,1)S(1)} copy(bf16[2,64,320]{2,1,0:T(8,128)(2,1)} %param.19) | data formatting | bytes 163840 | tf_op args[9]
  1.1 0.8 fusion.2
  2.0 0.1 copy.26
  2.1 0.1 copy.25
  2.2 0.1 maximum_bitcast_fusion
  2.3 0.7 pad_maximum_fusion.1.ad_ref
  3.7 0.0 copy-done
  3.8 0.6 reshape.8.mod_ref
  4.4 0.6 slice_bitcast_fusion.2.gate_ref
  5.0 1.1 %fusion.1 = (bf16[1,1920,64]{1,2,0:T(8,128)(2,1)S(1)}, bf16[1,1920,64]{1,2,0:T(8,128)(2,1)S(1)}) fusion(bf16[2,1920,64]{1,2,0:T(8,128)(2,1)} %param.18), kind=kLoop, calls=%fused_computation.10 | loop fusion | bytes 983040 | tf_op jit(solution)/shard_map/slice | solution.py:352
  6.1 0.3 copy.27
  6.4 0.3 copy.28
  6.7 1.1 %pad_maximum_fusion.di_ref = bf16[1920,128]{1,0:T(8,128)(2,1)} fusion(bf16[1920,64]{1,0:T(8,128)(2,1)S(1)} %bitcast.28, bf16[1920,64]{1,0:T(8,128)(2,1)S(1)} %bitcast.27), kind=kLoop, calls=%fused_computation | loop fusion | flops 983040 | bytes 983040 | tf_op jit(solution)/shard_map/concatenate | solution.py:352
  8.4 82.6 %shard_map.100 = bf16[64,1280]{1,0:T(8,128)(2,1)} custom-call(f32[1]{0:T(128)S(6)} %convert_element_type.9.keep_ref, bf16[64,1280]{1,0:T(8,128)(2,1)} %bitcast.34, f32[40,128]{1,0:T(8,128)} %reshape.8.mod_ref, f32[2,1280]{1,0:T(2,128)} %slice_bitcast_fusion.2.gate_ref, bf16[2,320,128]{2,1,0:T(8,128)(2,1)} %pad_maximum_fusion.1.ad_ref, ...), custom_call_target="tpu_custom_call" | custom-call | flops 8000000000 | bytes 80000000 | tf_op jit(solution)/shard_map/pallas_call | solution.py:359
  91.0 1.6 %copy.35 = bf16[1,64,1280]{2,1,0:T(8,128)(2,1)} copy(bf16[1,64,1280]{2,1,0:T(8,128)(2,1)} %bitcast.29) | data formatting | bytes 327680
  (5 shorter events, 0.1 us)
Async XLA Ops:
  0.0 3.7 %copy-start = (bf16[2,8,3,1280]{3,1,2,0:T(8,128)(2,1)S(1)}, bf16[2,8,3,1280]{3,1,2,0:T(8,128)(2,1)}, u32[]{:S(2)}) copy-start(bf16[2,8,3,1280]{3,1,2,0:T(8,128)(2,1)} %param.11) | copy-start | bytes 368644

commit v2 on v1

--- a/solution.py
+++ b/solution.py
@@ -118,13 +118,13 @@
 
 def window_kernel(
     n, nb,
-    keep_ref, lat_ref, mod_ref, gate_ref, ad_ref, uo_ref, di_ref, uw, dw,
+    keep_ref, step_ref, lat_ref, table_ref, ad_ref, uo_ref, di_ref, uw, dw,
     out_ref,
-    rows_all, mod_all, stat_all, low_all, back_all, ad_all, sums_in, sums_out,
+    rows_all, mod_mine, gates, mod_all, stat_all, low_all, back_all, ad_all, sums_in, sums_out,
     normed, act, hid, own, stat_mine, low_mine, back_mine,
     up_buf, down_buf,
     up_sem, down_sem,
-    rows_s, rows_r, mod_s, mod_r, stat_s, stat_r, low_s, low_r, back_s, back_r, ad_s, ad_r, sum_s, sum_r,
+    rows_s, rows_r, mod_s, mod_r, stat_s, stat_r, low_s, low_r, back_s, back_r, ad_s, ad_r, sum_s, sum_r, left_s,
 ):
     me = lax.axis_index(T_NAME)
     mb = lax.axis_index(B_NAME)
@@ -136,11 +136,12 @@
     keep = keep_ref[0]
     f32, bf16 = jnp.float32, jnp.bfloat16
 
-    def up_copy(level, step):
-        chunk = level * n + step
-        block = lax.rem(me + n - step, n)
+    def up_slot(level, block):
+        return lax.rem(level * n + block, up_slots)
+
+    def up_copy(level, block):
         rows = pl.ds(pl.multiple_of(block * width, LANES), width)
-        return pltpu.make_async_copy(uw.at[level, rows, :], up_buf.at[chunk % up_slots], up_sem.at[chunk])
+        return pltpu.make_async_copy(uw.at[level, rows, :], up_buf.at[up_slot(level, block)], up_sem.at[level * n + block])
 
     def down_copy(level, step):
         block = lax.rem(me + 1 + step, n)
@@ -148,7 +149,7 @@
         return pltpu.make_async_copy(dw.at[level, :, columns], down_buf.at[step], down_sem.at[level * n + step])
 
     for step in range(n):
-        up_copy(0, step).start()
+        up_copy(0, lax.rem(me + step, n)).start()
     for step in range(n):
         down_copy(0, step).start()
     for step in range(up_slots - n):
@@ -168,6 +169,67 @@
             src_ref=buf, dst_ref=buf, send_sem=r, recv_sem=r,
             device_id={T_NAME: lax.rem(me + 1, n)}, device_id_type=pl.DeviceIdType.MESH).wait_recv()
 
+    def relay(kind, hop, right):
+        block, target = (me - hop, me + 1) if right else (me + hop, me - 1)
+        return pltpu.make_async_remote_copy(
+            src_ref=rows_all.at[kind, block], dst_ref=rows_all.at[kind, block],
+            send_sem=rows_s.at[kind, block], recv_sem=rows_r.at[kind, block],
+            device_id={T_NAME: target}, device_id_type=pl.DeviceIdType.MESH)
+
+    def comes(hop, right):
+        return me >= hop if right else me + hop < n
+
+    def goes(hop, right):
+        return jnp.logical_and(me >= hop, me + 1 < n) if right else jnp.logical_and(me + hop < n, me > 0)
+
+    def own_rows(kind):
+        @pl.when(me + 1 < n)
+        def _():
+            relay(kind, 0, True).start()
+
+        @pl.when(me > 0)
+        def _():
+            pltpu.make_async_remote_copy(
+                src_ref=rows_all.at[kind, me], dst_ref=rows_all.at[kind, me],
+                send_sem=left_s.at[kind], recv_sem=rows_r.at[kind, me],
+                device_id={T_NAME: me - 1}, device_id_type=pl.DeviceIdType.MESH).start()
+
+    def sent_rows(kind):
+        @pl.when(me + 1 < n)
+        def _():
+            relay(kind, 0, True).wait_send()
+
+        @pl.when(me > 0)
+        def _():
+            pltpu.make_async_remote_copy(
+                src_ref=rows_all.at[kind, me], dst_ref=rows_all.at[kind, me],
+                send_sem=left_s.at[kind], recv_sem=rows_r.at[kind, me],
+                device_id={T_NAME: me - 1}, device_id_type=pl.DeviceIdType.MESH).wait_send()
+
+        for hop in range(1, n):
+            for right in (True, False):
+                @pl.when(goes(hop, right))
+                def _():
+                    relay(kind, hop, right).wait_send()
+
+    def walk(kind, use):
+        use(me, True)
+        for hop in range(1, n):
+            for right in (True, False):
+                @pl.when(comes(hop, right))
+                def _():
+                    block = me - hop if right else me + hop
+                    arrive(rows_all.at[kind, block], rows_r.at[kind, block])
+
+                @pl.when(goes(hop, right))
+                def _():
+                    relay(kind, hop, right).start()
+
+            for right in (True, False):
+                @pl.when(comes(hop, right))
+                def _():
+                    use(me - hop if right else me + hop, False)
+
     def to_peers(src, dst, s, r):
         for step in range(1, n):
             send(src, dst, s.at[step], r.at[me], {T_NAME: lax.rem(me + step, n)})
@@ -177,7 +239,15 @@
             block = lax.rem(me + n - step, n)
             arrive(buf.at[block], r.at[block])
 
+    rows_all[0, me] = lat_ref[...]
     stat_mine[0] = pack_moments(lat_ref[...].astype(f32))
+    for level in range(2):
+        rows = sum(jnp.where(step_ref[0] == s, table_ref[level, s].astype(f32), 0.0) for s in range(table_ref.shape[1]))
+        gates[level : level + 1, :] = rows[2:3]
+        for row in range(2):
+            for j in range(lane_rows):
+                place = (2 * level + row) * lane_rows + j
+                mod_mine[place : place + 1, :] = rows[row : row + 1, j * LANES : (j + 1) * LANES]
     barrier = pltpu.get_barrier_semaphore()
     for step in range(1, n):
         pl.semaphore_signal(barrier, inc=1, device_id={T_NAME: lax.rem(me + step, n)}, device_id_type=pl.DeviceIdType.MESH)
@@ -186,16 +256,15 @@
     pl.semaphore_wait(barrier, n - 1 + nb - 1)
 
     to_peers(stat_mine.at[0], stat_all.at[0, me], stat_s.at[0], stat_r.at[0])
-    to_peers(mod_ref, mod_all.at[me], mod_s, mod_r)
-    to_peers(lat_ref, rows_all.at[0, me], rows_s.at[0], rows_r.at[0])
+    to_peers(mod_mine, mod_all.at[me], mod_s, mod_r)
+    own_rows(0)
     spot = pl.ds(pl.multiple_of(mb * part, 16), part)
     for level in range(2):
         for step in range(1, nb):
             send(ad_ref.at[level], ad_all.at[level, spot, :], ad_s.at[level, step], ad_r.at[level, mb], {B_NAME: lax.rem(mb + step, nb)})
-    mod_all[me] = mod_ref[...]
+    mod_all[me] = mod_mine[...]
     ad_all[:, spot, :] = ad_ref[...]
     stat_all[0, me] = stat_mine[0]
-    rows_all[0, me] = lat_ref[...]
 
     def wait_ad(level):
         for step in range(1, nb):
@@ -237,12 +306,12 @@
     half = lax.broadcasted_iota(jnp.int32, (count, LANES), 1) < LANES // 2
 
     def low_sum(kind):
-        return sum(low_all[kind, b] for b in range(n))
+        return sum(low_all[kind, b].astype(f32) for b in range(n))
 
     def back_projection(level):
-        value = jnp.dot(act[...], di_ref[...], preferred_element_type=f32)
+        value = jnp.dot(act[...], di_ref[level], preferred_element_type=f32)
         mine = half if level == 1 else jnp.logical_not(half)
-        back_mine[level] = jnp.where(mine, value, 0.0)
+        back_mine[level] = jnp.where(mine, jnp.concatenate([value, value], axis=1), 0.0).astype(bf16)
         back_all[level, me] = back_mine[level]
         to_peers(back_mine.at[level], back_all.at[level, me], back_s.at[level], back_r.at[level])
 
@@ -261,12 +330,14 @@
             matmul_tiles(width, 256, body)
             if step < n - 1:
                 send(sums_out.at[level, step], sums_in.at[level, me], sum_s.at[level, step], sum_r.at[level, me], {T_NAME: lax.rem(me + 1 + step, n)})
+            if step == 0:
+                back_projection(level)
             if level == 0:
                 down_copy(1, step).start()
 
     def settle(level):
         from_peers(back_all.at[level], back_r.at[level])
-        low = sum(back_all[level, b] for b in range(n)).astype(bf16)
+        low = sum(back_all[level, b].astype(f32) for b in range(n)).astype(bf16)
         total = own[...] + lax.dot_general(low, ad_all[level], (((1,), (1,)), ((), ())), preferred_element_type=f32)
         from_peers(sums_in.at[level], sum_r.at[level])
         for step in range(1, n):
@@ -280,59 +351,57 @@
     low0 = jnp.dot(apply(0, 0, me, lat_stats), ad_all[0], preferred_element_type=f32)
     wait_ad(1)
     low1 = jnp.dot(apply(0, 1, me, lat_stats), ad_all[1], preferred_element_type=f32)
-    low_mine[0] = jnp.where(half, low0, low1)
+    low_mine[0] = jnp.where(half, low0, low1).astype(bf16)
     low_all[0, me] = low_mine[0]
     to_peers(low_mine.at[0], low_all.at[0, me], low_s.at[0], low_r.at[0])
-    for step in range(n):
-        block = lax.rem(me + n - step, n)
-        if step:
-            arrive(rows_all.at[0, block], rows_r.at[0, block])
+
+    def use_latent(block, init):
         normed[...] = apply(0, 0, block, lat_stats)
-        up_copy(0, step).wait()
-        up_step(step, 0, step == 0)
-        later = up_slots - n + step
-        if later < n:
-            up_copy(1, later).start()
+        up_copy(0, block).wait()
+        up_step(up_slot(0, block), 0, init)
+
+    walk(0, use_latent)
+    for block in range(up_slots - n, n):
+        up_copy(1, block).start()
     from_peers(low_all.at[0], low_r.at[0])
     add_low(0, jnp.where(half, low_sum(0), 0.0).astype(bf16))
     act[...] = jax.nn.gelu(hid[0], approximate=True).astype(bf16)
-    back_projection(0)
     down_steps(0)
-    for step in range(n):
-        block = lax.rem(me + n - step, n)
+    for block in range(n):
         normed[...] = apply(0, 1, block, lat_stats)
-        up_copy(1, step).wait()
-        up_step((n + step) % up_slots, 1, step == 0)
+        up_copy(1, block).wait()
+        up_step((n + block) % up_slots, 1, block == 0)
     add_low(1, jnp.where(half, 0.0, low_sum(0)).astype(bf16))
     hid[1] = jax.nn.gelu(hid[1], approximate=True)
-    first = (lat_ref[...].astype(f32) + gate_ref[0:1, :] * settle(0)).astype(bf16)
+    first = (lat_ref[...].astype(f32) + gates[0:1, :] * settle(0)).astype(bf16)
     rows_all[1, me] = first
     stat_mine[1] = pack_moments(first.astype(f32))
     to_peers(stat_mine.at[1], stat_all.at[1, me], stat_s.at[1], stat_r.at[1])
-    to_peers(rows_all.at[1, me], rows_all.at[1, me], rows_s.at[1], rows_r.at[1])
+    own_rows(1)
     stat_all[1, me] = stat_mine[1]
     from_peers(stat_all.at[1], stat_r.at[1])
     stats = statistics(1)
     low = jnp.dot(apply(1, 1, me, stats), ad_all[1], preferred_element_type=f32)
-    low_mine[1] = jnp.where(half, 0.0, low)
+    low_mine[1] = jnp.where(half, 0.0, low).astype(bf16)
     low_all[1, me] = low_mine[1]
     to_peers(low_mine.at[1], low_all.at[1, me], low_s.at[1], low_r.at[1])
-    for step in range(n):
-        block = lax.rem(me + n - step, n)
-        if step:
-            arrive(rows_all.at[1, block], rows_r.at[1, block])
+
+    def use_first(block, init):
         normed[...] = apply(1, 1, block, stats)
-        up_step((n + step) % up_slots, 0, step == 0)
+        up_step(up_slot(1, block), 0, init)
+
+    walk(1, use_first)
     from_peers(low_all.at[1], low_r.at[1])
     add_low(0, low_sum(1).astype(bf16))
     active = jax.nn.gelu(hid[0], approximate=True)
     act[...] = ((1.0 + guide_weight) * active - (guide_weight * keep) * hid[1]).astype(bf16)
-    back_projection(1)
     down_steps(1)
     total = settle(1)
     first_value = rows_all[1, me].astype(f32)
     start = first_value + guide_weight * keep * (first_value - lat_ref[...].astype(f32))
-    out_ref[...] = (start + gate_ref[1:2, :] * total).astype(out_ref.dtype)
+    out_ref[...] = (start + gates[1:2, :] * total).astype(out_ref.dtype)
+    for kind in range(2):
+        sent_rows(kind)
     for copy in sent:
         copy.wait_send()
 
@@ -343,13 +412,9 @@
     count, width = tokens.shape
     units = up_weight.shape[2]
     keep = (skip_layer == 0).astype(f32)
-    mods = lax.dynamic_index_in_dim(mod_table, step_index[0], axis=1, keepdims=False).astype(f32)
     lane_rows = 4 * width // LANES
-    mod_packed = mods[:, :2].reshape(lane_rows, LANES)
-    gates = mods[:, 2]
     turned = jnp.swapaxes(down_out, 1, 2)
     ad = jnp.stack([jnp.concatenate([up_in[0], turned[0]], axis=1), jnp.concatenate([turned[1], up_in[1]], axis=1)])
-    di = jnp.concatenate([down_in[1], down_in[0]], axis=1)
     uo = up_out.reshape(LANES, units)
     up_slots = n + 2
     vmem = pl.BlockSpec(memory_space=pltpu.VMEM)
@@ -359,14 +424,16 @@
     return pl.pallas_call(
         functools.partial(window_kernel, n, nb),
         out_shape=jax.ShapeDtypeStruct((count, width), bf16),
-        in_specs=[pl.BlockSpec(memory_space=pltpu.SMEM)] + [vmem] * 6 + [hbm] * 2,
+        in_specs=[pl.BlockSpec(memory_space=pltpu.SMEM)] * 2 + [vmem] * 5 + [hbm] * 2,
         out_specs=vmem,
         scratch_shapes=[
             pltpu.VMEM((2, n, count, width), bf16),
+            pltpu.VMEM((lane_rows, LANES), f32),
+            pltpu.VMEM((8, width), f32),
             pltpu.VMEM((n, lane_rows, LANES), f32),
             pltpu.VMEM((2, n, 8, LANES), f32),
-            pltpu.VMEM((2, n, count, LANES), f32),
-            pltpu.VMEM((2, n, count, LANES), f32),
+            pltpu.VMEM((2, n, count, LANES), bf16),
+            pltpu.VMEM((2, n, count, LANES), bf16),
             pltpu.VMEM((2, part * nb, LANES), bf16),
             pltpu.VMEM((2, n, count, width), bf16),
             pltpu.VMEM((2, n - 1, count, width), bf16),
@@ -375,8 +442,8 @@
             pltpu.VMEM((2, count, units), f32),
             pltpu.VMEM((count, width), f32),
             pltpu.VMEM((2, 8, LANES), f32),
-            pltpu.VMEM((2, count, LANES), f32),
-            pltpu.VMEM((2, count, LANES), f32),
+            pltpu.VMEM((2, count, LANES), bf16),
+            pltpu.VMEM((2, count, LANES), bf16),
             pltpu.VMEM((up_slots, width, units), bf16),
             pltpu.VMEM((n, units, width), bf16),
             dma((2 * n,)), dma((2 * n,)),
@@ -387,10 +454,11 @@
             dma((2, n)), dma((2, n)),
             dma((2, nb)), dma((2, nb)),
             dma((2, n)), dma((2, n)),
+            dma((2,)),
         ],
         compiler_params=pltpu.CompilerParams(collective_id=0, has_side_effects=True, vmem_limit_bytes=63 * 2**20),
         cost_estimate=pl.CostEstimate(flops=8 * 10**9, bytes_accessed=80 * 10**6, transcendentals=400000),
-    )(keep, tokens, mod_packed, gates, ad, uo, di, up_weight, down_weight)[None]
+    )(keep, step_index, tokens, mod_table, ad, uo, down_in, up_weight, down_weight)[None]
 
 
 def solution(mesh):

time: 92.9 us -> 87.5 us (0.942)
  Pallas kernels: 82.6 us -> 77.3 us
  other arithmetic: 1.88 us -> 0.8 us
  local copies, waits for them, and re-layouts: 6.7 us -> 7.72 us
    pallas_call x1, Pallas kernels: 82.6 us -> 77.3 us  [per_device_fused(): pl.pallas_call(functools.partial(window_kernel, n, nb), out_shape=jax.Sha...]
    unnamed x8 -> x6, local copies, waits for them, and re-layouts: 3.49 us -> 6.87 us
    slice x3 -> x0, local copies, waits for them, and re-layouts: 1.11 us -> none  [the longest x1 1.1 us: per_device_fused(): di = jnp.concatenate([down_in[1], down_in[0]], axis=1)]
    concatenate x1 -> x0, other arithmetic: 1.06 us -> none  [per_device_fused(): di = jnp.concatenate([down_in[1], down_in[0]], axis=1)]
where the time goes in v2:
time: 87.5 us; the launch traced here: 87.2 us
  Pallas kernels  77.3 us (88%)
  local copies, waits for them, and re-layouts  7.72 us (9%)
  between operations  1.33 us (2%)
    pallas_call x1, Pallas kernels, per_device_fused(): pl.pallas_call(functools.partial(window_kernel, n, nb), out_shape=jax.Sha...  77.3 us
    unnamed x6, local copies, waits for them, and re-layouts  6.87 us

profile of v2, /device:TPU:0, one launch (start us, length us, event | category | flops | bytes accessed | tf_op | source)
XLA Modules:
  0.0 87.2 jit_solution(11800100167993701061)
XLA Ops:
  1.3 0.8 fusion
  2.1 0.1 copy.16
  2.3 0.1 copy.17
  2.4 1.6 %copy.14.table_ref = bf16[2,8,3,1280]{3,2,1,0:T(4,128)(2,1)} copy(bf16[2,8,3,1280]{3,1,2,0:T(8,128)(2,1)} %param.11) | data formatting | bytes 245760 | tf_op args[1]
  4.0 1.1 %copy.12 = bf16[2,64,320]{1,2,0:T(8,128)(2,1)S(1)} copy(bf16[2,64,320]{2,1,0:T(8,128)(2,1)} %param.19) | data formatting | bytes 163840 | tf_op args[9]
  5.1 0.1 maximum_bitcast_fusion
  5.2 0.7 pad_maximum_fusion.ad_ref
  5.9 2.3 %copy.15.di_ref = bf16[2,1920,64]{2,1,0:T(8,128)(2,1)} copy(bf16[2,1920,64]{1,2,0:T(8,128)(2,1)} %param.18) | data formatting | bytes 983040 | tf_op args[8]
  8.3 77.3 %shard_map.100 = bf16[64,1280]{1,0:T(8,128)(2,1)} custom-call(f32[1]{0:T(128)S(6)} %convert_element_type.3.keep_ref, s32[1]{0:T(128)S(6)} %copy.20.step_ref, bf16[64,1280]{1,0:T(8,128)(2,1)} %bitcast.19, bf16[2,8,3,1280]{3,2,1,0:T(4,128)(2,1)} %copy.14.table_ref, bf16[2,320,128]{2,1,0:T(8,128)(2,1)} %pad_maximum_fusion.ad_ref, bf16[128,1920]{1,0:T(8,128)(2,1)} %bitcast.16, ...), custom_call_target="tpu_custom_call" | custom-call | flops 8000000000 | bytes 80000000 | tf_op jit(solution)/shard_map/pallas_call | solution.py:424
  85.6 1.6 %copy.21 = bf16[1,64,1280]{2,1,0:T(8,128)(2,1)} copy(bf16[1,64,1280]{2,1,0:T(8,128)(2,1)} %bitcast.14) | data formatting | bytes 327680
  (1 shorter events, 0.0 us)

commit v3 on v2

--- a/solution.py
+++ b/solution.py
@@ -118,9 +118,9 @@
 
 def window_kernel(
     n, nb,
-    keep_ref, step_ref, lat_ref, table_ref, ad_ref, uo_ref, di_ref, uw, dw,
+    keep_ref, step_ref, lat_ref, table_ref, ui_ref, do_ref, uo_ref, di_ref, uw, dw,
     out_ref,
-    rows_all, mod_mine, gates, mod_all, stat_all, low_all, back_all, ad_all, sums_in, sums_out,
+    ad_ref, rows_all, mod_mine, gates, mod_all, stat_all, low_all, back_all, ad_all, sums_in, sums_out,
     normed, act, hid, own, stat_mine, low_mine, back_mine,
     up_buf, down_buf,
     up_sem, down_sem,
@@ -242,12 +242,15 @@
     rows_all[0, me] = lat_ref[...]
     stat_mine[0] = pack_moments(lat_ref[...].astype(f32))
     for level in range(2):
-        rows = sum(jnp.where(step_ref[0] == s, table_ref[level, s].astype(f32), 0.0) for s in range(table_ref.shape[1]))
-        gates[level : level + 1, :] = rows[2:3]
+        chosen = lax.broadcasted_iota(jnp.int32, table_ref.shape[2:], 0) == step_ref[0]
+        picked = [jnp.sum(jnp.where(chosen, table_ref[level, row].astype(f32), 0.0), axis=0, keepdims=True) for row in range(3)]
+        gates[level : level + 1, :] = picked[2]
+        both = [ui_ref[level].astype(f32), do_ref[level].astype(f32)]
+        ad_ref[level] = jnp.concatenate(both if level == 0 else both[::-1], axis=0).T.astype(bf16)
         for row in range(2):
             for j in range(lane_rows):
                 place = (2 * level + row) * lane_rows + j
-                mod_mine[place : place + 1, :] = rows[row : row + 1, j * LANES : (j + 1) * LANES]
+                mod_mine[place : place + 1, :] = picked[row][:, j * LANES : (j + 1) * LANES]
     barrier = pltpu.get_barrier_semaphore()
     for step in range(1, n):
         pl.semaphore_signal(barrier, inc=1, device_id={T_NAME: lax.rem(me + step, n)}, device_id_type=pl.DeviceIdType.MESH)
@@ -309,7 +312,7 @@
         return sum(low_all[kind, b].astype(f32) for b in range(n))
 
     def back_projection(level):
-        value = jnp.dot(act[...], di_ref[level], preferred_element_type=f32)
+        value = lax.dot_general(act[...], di_ref[level], (((1,), (1,)), ((), ())), preferred_element_type=f32)
         mine = half if level == 1 else jnp.logical_not(half)
         back_mine[level] = jnp.where(mine, jnp.concatenate([value, value], axis=1), 0.0).astype(bf16)
         back_all[level, me] = back_mine[level]
@@ -413,20 +416,19 @@
     units = up_weight.shape[2]
     keep = (skip_layer == 0).astype(f32)
     lane_rows = 4 * width // LANES
-    turned = jnp.swapaxes(down_out, 1, 2)
-    ad = jnp.stack([jnp.concatenate([up_in[0], turned[0]], axis=1), jnp.concatenate([turned[1], up_in[1]], axis=1)])
     uo = up_out.reshape(LANES, units)
     up_slots = n + 2
     vmem = pl.BlockSpec(memory_space=pltpu.VMEM)
     hbm = pl.BlockSpec(memory_space=pl.ANY)
     dma = pltpu.SemaphoreType.DMA
-    part = ad.shape[1]
+    part = up_in.shape[1]
     return pl.pallas_call(
         functools.partial(window_kernel, n, nb),
         out_shape=jax.ShapeDtypeStruct((count, width), bf16),
-        in_specs=[pl.BlockSpec(memory_space=pltpu.SMEM)] * 2 + [vmem] * 5 + [hbm] * 2,
+        in_specs=[pl.BlockSpec(memory_space=pltpu.SMEM)] * 2 + [vmem] * 6 + [hbm] * 2,
         out_specs=vmem,
         scratch_shapes=[
+            pltpu.VMEM((2, part, LANES), bf16),
             pltpu.VMEM((2, n, count, width), bf16),
             pltpu.VMEM((lane_rows, LANES), f32),
             pltpu.VMEM((8, width), f32),
@@ -458,7 +460,7 @@
         ],
         compiler_params=pltpu.CompilerParams(collective_id=0, has_side_effects=True, vmem_limit_bytes=63 * 2**20),
         cost_estimate=pl.CostEstimate(flops=8 * 10**9, bytes_accessed=80 * 10**6, transcendentals=400000),
-    )(keep, step_index, tokens, mod_table, ad, uo, down_in, up_weight, down_weight)[None]
+    )(keep, step_index, tokens, jnp.swapaxes(mod_table, 1, 2), jnp.swapaxes(up_in, 1, 2), down_out, uo, jnp.swapaxes(down_in, 1, 2), up_weight, down_weight)[None]
 
 
 def solution(mesh):

time: 87.5 us -> 80.3 us (0.918)
  local copies, waits for them, and re-layouts: 7.72 us -> 1.59 us
    unnamed x6 -> x1, local copies, waits for them, and re-layouts: 6.87 us -> 1.59 us
where the time goes in v3:
time: 80.3 us; the launch traced here: 80.1 us
  Pallas kernels  77.2 us (96%)
  local copies, waits for them, and re-layouts  1.59 us (2%)
  between operations  1.31 us (2%)
    pallas_call x1, Pallas kernels, per_device_fused(): pl.pallas_call(functools.partial(window_kernel, n, nb), out_shape=jax.Sha...  77.2 us

profile of v3, /device:TPU:0, one launch (start us, length us, event | category | flops | bytes accessed | tf_op | source)
XLA Modules:
  0.0 80.1 jit_solution(1472829385111287573)
XLA Ops:
  1.3 77.2 %shard_map.100 = bf16[64,1280]{1,0:T(8,128)(2,1)} custom-call(f32[1]{0:T(128)S(6)} %convert_element_type.3.keep_ref, s32[1]{0:T(128)S(6)} %copy.13.step_ref, bf16[64,1280]{1,0:T(8,128)(2,1)} %bitcast.9, bf16[2,3,8,1280]{3,2,1,0:T(8,128)(2,1)} %bitcast.10, bf16[2,64,320]{2,1,0:T(8,128)(2,1)} %bitcast.11, bf16[2,64,320]{2,1,0:T(8,128)(2,1)} %do_ref.1, ...), custom_call_target="tpu_custom_call" | custom-call | flops 8000000000 | bytes 80000000 | tf_op jit(solution)/shard_map/pallas_call | solution.py:425
  78.5 1.6 %copy.14 = bf16[1,64,1280]{2,1,0:T(8,128)(2,1)} copy(bf16[1,64,1280]{2,1,0:T(8,128)(2,1)} %bitcast.6) | data formatting | bytes 327680

commit v4 on v3

--- a/solution.py
+++ b/solution.py
@@ -212,7 +212,7 @@
                 def _():
                     relay(kind, hop, right).wait_send()
 
-    def walk(kind, use):
+    def walk(kind, use, between=None):
         use(me, True)
         for hop in range(1, n):
             for right in (True, False):
@@ -229,6 +229,9 @@
                 @pl.when(comes(hop, right))
                 def _():
                     use(me - hop if right else me + hop, False)
+
+            if hop == 1 and between is not None:
+                between()
 
     def to_peers(src, dst, s, r):
         for step in range(1, n):
@@ -350,20 +353,22 @@
     from_peers(stat_all.at[0], stat_r.at[0])
     from_peers(mod_all, mod_r)
     lat_stats = statistics(0)
-    wait_ad(0)
-    low0 = jnp.dot(apply(0, 0, me, lat_stats), ad_all[0], preferred_element_type=f32)
-    wait_ad(1)
-    low1 = jnp.dot(apply(0, 1, me, lat_stats), ad_all[1], preferred_element_type=f32)
-    low_mine[0] = jnp.where(half, low0, low1).astype(bf16)
-    low_all[0, me] = low_mine[0]
-    to_peers(low_mine.at[0], low_all.at[0, me], low_s.at[0], low_r.at[0])
+
+    def low_latent():
+        wait_ad(0)
+        low0 = jnp.dot(apply(0, 0, me, lat_stats), ad_all[0], preferred_element_type=f32)
+        wait_ad(1)
+        low1 = jnp.dot(apply(0, 1, me, lat_stats), ad_all[1], preferred_element_type=f32)
+        low_mine[0] = jnp.where(half, low0, low1).astype(bf16)
+        low_all[0, me] = low_mine[0]
+        to_peers(low_mine.at[0], low_all.at[0, me], low_s.at[0], low_r.at[0])
 
     def use_latent(block, init):
         normed[...] = apply(0, 0, block, lat_stats)
         up_copy(0, block).wait()
         up_step(up_slot(0, block), 0, init)
 
-    walk(0, use_latent)
+    walk(0, use_latent, low_latent)
     for block in range(up_slots - n, n):
         up_copy(1, block).start()
     from_peers(low_all.at[0], low_r.at[0])

time: 80.3 us -> 74.6 us (0.929)
  Pallas kernels: 77.2 us -> 71.6 us
    pallas_call x1, Pallas kernels: 77.2 us -> 71.6 us  [per_device_fused(): pl.pallas_call(functools.partial(window_kernel, n, nb), out_shape=jax.Sha...]
where the time goes in v4:
time: 74.6 us; the launch traced here: 74.5 us
  Pallas kernels  71.6 us (96%)
  local copies, waits for them, and re-layouts  1.59 us (2%)
  between operations  1.31 us (2%)
    pallas_call x1, Pallas kernels, per_device_fused(): pl.pallas_call(functools.partial(window_kernel, n, nb), out_shape=jax.Sha...  71.6 us
    unnamed x1, local copies, waits for them, and re-layouts  1.59 us

profile of v4, /device:TPU:0, one launch (start us, length us, event | category | flops | bytes accessed | tf_op | source)
XLA Modules:
  0.0 74.5 jit_solution(9134537601579050555)
XLA Ops:
  1.3 71.6 %shard_map.100 = bf16[64,1280]{1,0:T(8,128)(2,1)} custom-call(f32[1]{0:T(128)S(6)} %convert_element_type.3.keep_ref, s32[1]{0:T(128)S(6)} %copy.13.step_ref, bf16[64,1280]{1,0:T(8,128)(2,1)} %bitcast.9, bf16[2,3,8,1280]{3,2,1,0:T(8,128)(2,1)} %bitcast.10, bf16[2,64,320]{2,1,0:T(8,128)(2,1)} %bitcast.11, bf16[2,64,320]{2,1,0:T(8,128)(2,1)} %do_ref.1, ...), custom_call_target="tpu_custom_call" | custom-call | flops 8000000000 | bytes 80000000 | tf_op jit(solution)/shard_map/pallas_call | solution.py:430
  72.9 1.6 %copy.14 = bf16[1,64,1280]{2,1,0:T(8,128)(2,1)} copy(bf16[1,64,1280]{2,1,0:T(8,128)(2,1)} %bitcast.6) | data formatting | bytes 327680
